TPU v7x, 256 devices: a whole 4x4x8 slice. The times are simulated.
256 devices in a mesh: section: 2 (over x_lo), row: 4 (over x_hi, core), col: 32 (over z, y).
Axes of the slice: x: 4 (x_hi: 2, x_lo: 2; x = x_hi * 2 + x_lo), y: 4, z: 8, core: 2. Of those that a mesh axis runs over, the one named last changes fastest.
Arguments:
- tokens: bfloat16 [1024, 4096], P('col', 'row'), may hold values from -6 to 6
- w_up: bfloat16 [2, 4096, 16384], P('section', 'row', 'col'), may hold values from -0.09375 to 0.09375
- w_down: bfloat16 [2, 16384, 4096], P('section', 'col', 'row'), may hold values from -0.046875 to 0.046875
- cotangent: bfloat16 [1024, 4096], P('row'), may hold values from -0.23925781 to 0.23925781
Outputs:
- grad_up: float32 [2, 4096, 16384], P('section', 'row', 'col')
- grad_down: float32 [2, 16384, 4096], P('section', 'col', 'row')
All inputs are finite; a program needn't handle non-finite values.
Results may differ from a plain program's by a relative error of at most 0.025.
Values may be sent and summed in bfloat16 or wider, within the bound.
No kernel may reach another device: no remote copies, remote signals or barrier semaphores. Data moves between devices by JAX's collectives and lax.ppermute only.
A program may use at most 128 MiB of HBM per device.

v0:
```python
import jax
import jax.numpy as jnp
from jax import lax
from jax.sharding import PartitionSpec as P


def from_behind(value, axis, by):
    devices = lax.axis_size(axis)
    pairs = [(i, i + by) for i in range(devices) if 0 <= i + by < devices]
    return lax.ppermute(value, axis, pairs)


def gelu(values):
    return jax.nn.gelu(values, approximate=True)


def gelu_grad(values, upstream):
    return jax.vjp(gelu, values)[1](upstream)[0]


def contract_rows(left, right):
    return lax.dot_general(
        left, right, (((0,), (0,)), ((), ())), preferred_element_type=jnp.float32
    )


def contract_cols(left, right):
    return lax.dot_general(
        left, right, (((1,), (1,)), ((), ())), preferred_element_type=jnp.float32
    )


def gated(flag, compute, shape):
    return lax.cond(flag, compute, lambda: jnp.zeros(shape, jnp.float32))


def body(tokens, w_up, w_down, cotangent):
    first_section = lax.axis_index("section") == 0
    second_section = jnp.logical_not(first_section)
    up_local = w_up[0]
    down_local = w_down[0]
    slice_tokens, feat_width = tokens.shape
    hidden_width = up_local.shape[1]
    block_tokens, model_width = cotangent.shape
    whole_tokens = lax.all_gather(tokens, "col", axis=0, tiled=True)
    all_tokens = whole_tokens.shape[0]
    pre_part = gated(
        first_section,
        lambda: jnp.dot(whole_tokens, up_local, preferred_element_type=jnp.float32),
        (all_tokens, hidden_width),
    )
    pre_a = lax.psum(pre_part.astype(jnp.bfloat16), "row").astype(jnp.float32)
    hidden_a = gelu(pre_a).astype(jnp.bfloat16)
    out_part = gated(
        first_section,
        lambda: jnp.dot(hidden_a, down_local, preferred_element_type=jnp.float32),
        (all_tokens, feat_width),
    )
    out_sum = lax.psum(out_part.astype(jnp.bfloat16), "col").astype(jnp.float32)
    boundary_a = (whole_tokens + out_sum).astype(jnp.bfloat16)
    boundary_feat = from_behind(boundary_a, "section", 1)
    boundary_b = lax.all_to_all(boundary_feat, "row", split_axis=0, concat_axis=1, tiled=True)
    up_full, down_full = (
        lax.all_gather(up_local, "row", axis=0, tiled=True),
        lax.all_gather(down_local, "row", axis=1, tiled=True),
    )
    pre_b = gated(
        second_section,
        lambda: jnp.dot(boundary_b, up_full, preferred_element_type=jnp.float32),
        (block_tokens, hidden_width),
    )
    hidden_b = gelu(pre_b).astype(jnp.bfloat16)
    grad_hidden_b = gated(
        second_section, lambda: contract_cols(cotangent, down_full), (block_tokens, hidden_width)
    )
    grad_pre_b = gelu_grad(pre_b, grad_hidden_b).astype(jnp.bfloat16)
    down_term = gated(
        second_section, lambda: contract_rows(cotangent, hidden_b), (model_width, hidden_width)
    )
    up_term = gated(
        second_section, lambda: contract_rows(boundary_b, grad_pre_b), (model_width, hidden_width)
    )
    down_scattered, up_b = (
        lax.psum_scatter(
            down_term.astype(jnp.bfloat16), "row", scatter_dimension=0, tiled=True
        ).astype(jnp.float32),
        lax.psum_scatter(
            up_term.astype(jnp.bfloat16), "row", scatter_dimension=0, tiled=True
        ).astype(jnp.float32),
    )
    down_b = down_scattered.T
    back_rows, back_width = cotangent.shape
    back_sum = lax.psum(
        gated(
            second_section, lambda: contract_cols(grad_pre_b, up_full), (back_rows, back_width)
        ).astype(jnp.bfloat16),
        "col",
    ).astype(jnp.float32)
    grad_boundary_b = (cotangent + back_sum).astype(jnp.bfloat16)
    returned = from_behind(grad_boundary_b, "section", -1)
    grad_boundary = lax.all_to_all(returned, "row", split_axis=1, concat_axis=0, tiled=True)
    hidden_part = gated(
        first_section, lambda: contract_cols(grad_boundary, down_local), (all_tokens, hidden_width)
    )
    grad_hidden_a = lax.psum(hidden_part.astype(jnp.bfloat16), "row").astype(jnp.float32)
    grad_pre_a = gelu_grad(pre_a, grad_hidden_a).astype(jnp.bfloat16)
    down_a = gated(
        first_section, lambda: contract_rows(hidden_a, grad_boundary), (hidden_width, feat_width)
    )
    up_a = gated(
        first_section, lambda: contract_rows(whole_tokens, grad_pre_a), (feat_width, hidden_width)
    )
    grad_up = jnp.where(first_section, up_a, up_b)[None]
    grad_down = jnp.where(first_section, down_a, down_b)[None]
    return (grad_up, grad_down)


def solution(mesh):
    placed = (
        P("col", "row"),
        P("section", "row", "col"),
        P("section", "col", "row"),
        P("row", None),
    )
    return jax.shard_map(
        body,
        mesh=mesh,
        in_specs=placed,
        out_specs=(P("section", "row", "col"), P("section", "col", "row")),
        check_vma=False,
    )
```

profile of v0, /device:TPU:1, one launch (start us, length us, event | category | flops | bytes accessed | tf_op | source)
XLA Modules:
  0.0 852.7 jit_solution(11803876582007134094)
XLA Ops:
  7.2 0.0 all-gather.6.cloned.1.call-start
  7.2 0.7 all-gather.6.cloned.1.call-update
  7.9 0.0 all-reduce.5.cloned.1.call-start
  8.0 80.5 %all-gather.6.cloned.1.call-done = bf16[1024,1024]{1,0:T(8,128)(2,1)} async-done(((bf16[32,1024]{1,0:T(8,128)(2,1)}), bf16[1024,1024]{1,0:T(8,128)(2,1)}) %all-gather.6.cloned.1.call-update) | async-done | bytes 2097168 | tf_op jit(solution)/shard_map/all_gather | solution.py:45
  88.5 3.1 conditional.11
  88.5 3.1 fusion.16
  91.6 0.9 copy-done.4
  92.5 0.0 all-reduce.5.cloned.1.call-update
  92.6 0.0 all-reduce.7.cloned.1.call-start
  92.6 51.9 %all-reduce.5.cloned.1.call-done = bf16[1024,512]{1,0:T(8,128)(2,1)} async-done(((bf16[1024,512]{1,0:T(8,128)(2,1)}), bf16[1024,512]{1,0:T(8,128)(2,1)}) %all-reduce.5.cloned.1.call-update) | async-done | bytes 1048592 | tf_op jit(solution)/shard_map/psum | solution.py:52
  144.6 2.9 fusion.8
  147.5 2.5 conditional.12
  147.5 2.5 fusion.17
  150.0 1.3 copy-done.2
  151.3 0.0 all-reduce.7.cloned.1.call-update
  151.3 0.0 all-gather.8.cloned.1.call-start
  151.3 0.5 all-gather.8.cloned.1.call-update
  151.9 0.0 all-gather.10.cloned.1.call-start
  151.9 0.5 all-gather.10.cloned.1.call-update
  152.5 148.3 %all-reduce.7.cloned.1.call-done = bf16[1024,1024]{1,0:T(8,128)(2,1)} async-done(((bf16[1024,1024]{1,0:T(8,128)(2,1)}), bf16[1024,1024]{1,0:T(8,128)(2,1)}) %all-reduce.7.cloned.1.call-update) | async-done | bytes 2097168 | tf_op jit(solution)/shard_map/psum | solution.py:59
  300.7 3.2 add_convert_fusion.1
  303.9 3.2 collective-permute-start
  307.1 62.1 %collective-permute-done = bf16[1024,1024]{1,0:T(8,128)(2,1)S(1)} collective-permute-done((bf16[1024,1024]{1,0:T(8,128)(2,1)S(1)}, bf16[1024,1024]{1,0:T(8,128)(2,1)S(1)}, u32[]{:S(2)}, u32[]{:S(2)}) %collective-permute-start) | collective-permute-done | bytes 2097184 | tf_op jit(solution)/shard_map/ppermute | solution.py:10
  369.2 1.3 copy-done.6
  370.5 10.6 %all-to-all-start = ((bf16[4,256,1024]{2,1,0:T(8,128)(2,1)}), bf16[4,256,1024]{2,1,0:T(8,128)(2,1)}, u32[]{:S(2)}, u32[]{:S(2)}) async-start(bf16[4,256,1024]{2,1,0:T(8,128)(2,1)} %bitcast.48), calls=%async_computation | async-start | bytes 4194304 | tf_op jit(solution)/shard_map/all_to_all | solution.py:62
  381.2 0.1 conditional.10
  381.2 0.1 broadcast.41
  381.3 48.9 %all-to-all-done = bf16[4,256,1024]{2,1,0:T(8,128)(2,1)} async-done(((bf16[4,256,1024]{2,1,0:T(8,128)(2,1)}), bf16[4,256,1024]{2,1,0:T(8,128)(2,1)}, u32[]{:S(2)}, u32[]{:S(2)}) %all-to-all-start) | async-done | bytes 2097184 | tf_op jit(solution)/shard_map/all_to_all | solution.py:62
  430.2 2.9 copy.11
  433.1 0.0 all-gather.10.cloned.1.call-done
  433.1 0.1 conditional.13
  433.1 0.1 broadcast.44
  433.2 0.1 broadcast.44.clone
  433.3 2.1 multiply_convert_fusion
  435.4 1.6 conditional.14
  435.4 1.6 broadcast.45
  436.9 152.8 %all-reduce.9.cloned.1.call-done = bf16[256,4096]{1,0:T(8,128)(2,1)} async-done(((bf16[256,4096]{1,0:T(8,128)(2,1)}), bf16[256,4096]{1,0:T(8,128)(2,1)}) %all-reduce.9.cloned.1.call-update) | async-done | bytes 2097168 | tf_op jit(solution)/shard_map/psum | solution.py:93
  589.8 3.0 add_convert_fusion
  592.8 1.3 collective-permute-start.1
  594.1 42.5 %collective-permute-done.1 = bf16[256,4096]{1,0:T(8,128)(2,1)S(1)} collective-permute-done((bf16[256,4096]{1,0:T(8,128)(2,1)S(1)}, bf16[256,4096]{1,0:T(8,128)(2,1)S(1)}, u32[]{:S(2)}, u32[]{:S(2)}) %collective-permute-start.1) | collective-permute-done | bytes 2097184 | tf_op jit(solution)/shard_map/ppermute | solution.py:10
  636.6 1.5 copy.20
  638.1 10.5 %all-to-all-start.1 = ((bf16[256,4,1024]{2,0,1:T(8,128)(2,1)}), bf16[256,4,1024]{2,0,1:T(8,128)(2,1)}, u32[]{:S(2)}, u32[]{:S(2)}) async-start(bf16[256,4,1024]{2,0,1:T(8,128)(2,1)} %bitcast.45), calls=%async_computation.1 | async-start | bytes 4194304 | tf_op jit(solution)/shard_map/all_to_all | solution.py:101
  648.7 26.4 %all-to-all-done.1 = bf16[256,4,1024]{2,0,1:T(8,128)(2,1)} async-done(((bf16[256,4,1024]{2,0,1:T(8,128)(2,1)}), bf16[256,4,1024]{2,0,1:T(8,128)(2,1)}, u32[]{:S(2)}, u32[]{:S(2)}) %all-to-all-start.1) | async-done | bytes 2097184 | tf_op jit(solution)/shard_map/all_to_all | solution.py:101
  675.1 3.1 conditional.15
  675.1 3.1 fusion.19
  678.3 1.0 copy-done.5
  679.2 0.0 reduce-scatter.3.cloned.1.call-start
  679.3 2.5 conditional.17
  679.5 2.3 broadcast.48
  681.8 0.0 reduce-scatter.5.cloned.1.call-start
  681.9 1.5 copy-done.1
  683.4 2.3 conditional.19
  683.4 2.3 broadcast.50
  685.7 6.5 copy.15
  692.2 3.3 conditional.18
  692.2 3.3 fusion.22
  695.5 30.0 %all-reduce.11.cloned.1.call-done = bf16[1024,512]{1,0:T(8,128)(2,1)} async-done(((bf16[1024,512]{1,0:T(8,128)(2,1)}), bf16[1024,512]{1,0:T(8,128)(2,1)}) %all-reduce.11.cloned.1.call-update) | async-done | bytes 1048592 | tf_op jit(solution)/shard_map/psum | solution.py:105
  725.5 3.7 fusion.3
  729.3 4.5 conditional.16
  729.3 4.5 fusion.20
  733.7 50.6 %reduce-scatter.3.cloned.1.call-done = bf16[1024,512]{1,0:T(8,128)(2,1)} async-done(((bf16[4096,512]{1,0:T(8,128)(2,1)}), bf16[1024,512]{1,0:T(8,128)(2,1)}) %reduce-scatter.3.cloned.1.call-update) | async-done | bytes 1048592 | tf_op jit(solution)/shard_map/reduce_scatter | solution.py:87
  784.3 3.5 select_bitcast_fusion
  787.8 55.6 %reduce-scatter.5.cloned.1.call-done = bf16[1024,512]{0,1:T(8,128)(2,1)} async-done(((bf16[4096,512]{0,1:T(8,128)(2,1)}), bf16[1024,512]{0,1:T(8,128)(2,1)}) %reduce-scatter.5.cloned.1.call-update) | async-done | bytes 1048592 | tf_op jit(solution)/shard_map/reduce_scatter | solution.py:84
  843.4 2.8 fusion.11
  (22 shorter events, 0.1 us)
Async XLA Ops:
  7.2 81.3 %all-gather.6.cloned.1.call-start = ((), (), s32[]{:S(2)}) async-start(), calls=%async_computation.4 | async-start | bytes 2162688 | tf_op jit(solution)/shard_map/all_gather | solution.py:45
  7.9 136.7 %all-reduce.5.cloned.1.call-start = ((), (), s32[]{:S(2)}) async-start(), calls=%async_computation.5 | async-start | bytes 2097152 | tf_op jit(solution)/shard_map/psum | solution.py:52
  91.6 1.0 copy-start.4
  91.6 55.9 %copy-start.8 = (bf16[1,512,1024]{2,1,0:T(8,128)(2,1)S(1)}, bf16[1,512,1024]{2,1,0:T(8,128)(2,1)}, u32[]{:S(2)}) copy-start(bf16[1,512,1024]{2,1,0:T(8,128)(2,1)} %param.26) | copy-start | bytes 3145732
  92.6 208.1 %all-reduce.7.cloned.1.call-start = ((), (), s32[]{:S(2)}) async-start(), calls=%async_computation.6 | async-start | bytes 4194304 | tf_op jit(solution)/shard_map/psum | solution.py:59
  149.9 1.3 copy-start.2
  151.3 229.9 %all-gather.8.cloned.1.call-start = ((), (), s32[]{:S(2)}) async-start(), calls=%async_computation.11 | async-start | bytes 5242880 | tf_op jit(solution)/shard_map/all_gather | solution.py:65
  151.9 281.2 %all-gather.10.cloned.1.call-start = ((), (), s32[]{:S(2)}) async-start(), calls=%async_computation.12 | async-start | bytes 5242880 | tf_op jit(solution)/shard_map/all_gather | solution.py:64
  303.9 65.3 %collective-permute-start = (bf16[1024,1024]{1,0:T(8,128)(2,1)S(1)}, bf16[1024,1024]{1,0:T(8,128)(2,1)S(1)}, u32[]{:S(2)}, u32[]{:S(2)}) collective-permute-start(bf16[1024,1024]{1,0:T(8,128)(2,1)S(1)} %add_convert_fusion.1), channel_id=1, source_target_pairs={{0,128},{1,129},{2,130},{3,131},{4,132},{5,133},{6,134},{7,135},{8... | collective-permute-start | bytes 6291464 | tf_op jit(solution)/shard_map/ppermute | solution.py:10
  369.2 1.3 copy-start.6
  370.5 10.7 %copy-start = (bf16[256,4096]{1,0:T(8,128)(2,1)S(1)}, bf16[256,4096]{1,0:T(8,128)(2,1)}, u32[]{:S(2)}) copy-start(bf16[256,4096]{1,0:T(8,128)(2,1)} %param.27) | copy-start | bytes 6291460
  370.5 59.7 %all-to-all-start = ((bf16[4,256,1024]{2,1,0:T(8,128)(2,1)}), bf16[4,256,1024]{2,1,0:T(8,128)(2,1)}, u32[]{:S(2)}, u32[]{:S(2)}) async-start(bf16[4,256,1024]{2,1,0:T(8,128)(2,1)} %bitcast.48), calls=%async_computation | async-start | bytes 4194304 | tf_op jit(solution)/shard_map/all_to_all | solution.py:62
  381.2 208.6 %all-reduce.9.cloned.1.call-start = ((), (), s32[]{:S(2)}) async-start(), calls=%async_computation.7 | async-start | bytes 4194304 | tf_op jit(solution)/shard_map/psum | solution.py:93
  381.3 51.8 %copy-start.7 = (f32[256,512]{1,0:T(8,128)}, f32[256,512]{1,0:T(8,128)S(1)}, u32[]{:S(2)}) copy-start(f32[256,512]{1,0:T(8,128)S(1)} %get-tuple-element.107) | copy-start | bytes 1572868
  592.8 43.8 %collective-permute-start.1 = (bf16[256,4096]{1,0:T(8,128)(2,1)S(1)}, bf16[256,4096]{1,0:T(8,128)(2,1)S(1)}, u32[]{:S(2)}, u32[]{:S(2)}) collective-permute-start(bf16[256,4096]{1,0:T(8,128)(2,1)S(1)} %add_convert_fusion), channel_id=1, source_target_pairs={{128,0},{129,1},{130,2},{131,3},{132,4},{133,5},{134,6},{135,7},{1... | collective-permute-start | bytes 6291464 | tf_op jit(solution)/shard_map/ppermute | solution.py:10
  638.1 37.0 %all-to-all-start.1 = ((bf16[256,4,1024]{2,0,1:T(8,128)(2,1)}), bf16[256,4,1024]{2,0,1:T(8,128)(2,1)}, u32[]{:S(2)}, u32[]{:S(2)}) async-start(bf16[256,4,1024]{2,0,1:T(8,128)(2,1)} %bitcast.45), calls=%async_computation.1 | async-start | bytes 4194304 | tf_op jit(solution)/shard_map/all_to_all | solution.py:101
  648.7 76.9 %all-reduce.11.cloned.1.call-start = ((), (), s32[]{:S(2)}) async-start(), calls=%async_computation.8 | async-start | bytes 2097152 | tf_op jit(solution)/shard_map/psum | solution.py:105
  678.2 1.0 copy-start.5
  679.2 105.1 %reduce-scatter.3.cloned.1.call-start = ((), (), s32[]{:S(2)}) async-start(), calls=%async_computation.9 | async-start | bytes 5242880 | tf_op jit(solution)/shard_map/reduce_scatter | solution.py:87
  681.8 1.6 copy-start.1
  681.8 1.6 copy-start.9
  681.8 161.6 %reduce-scatter.5.cloned.1.call-start = ((), (), s32[]{:S(2)}) async-start(), calls=%async_computation.10 | async-start | bytes 5242880 | tf_op jit(solution)/shard_map/reduce_scatter | solution.py:84
  692.2 33.3 %copy-start.3 = (bf16[1024,512]{1,0:T(8,128)(2,1)S(1)}, bf16[1024,512]{1,0:T(8,128)(2,1)}, u32[]{:S(2)}) copy-start(bf16[1024,512]{1,0:T(8,128)(2,1)} %all-reduce.5.cloned.1.call-done) | copy-start | bytes 3145732
Sparse Core Ops, SparseCore 0:
  10.6 77.8 all-gather.5
  92.7 51.8 all-reduce.4
  151.4 149.2 all-reduce.6
  302.4 65.3 all-gather.7
  369.5 62.3 all-gather.9
  437.1 152.6 all-reduce.8
  679.4 46.1 all-reduce.10
  728.3 55.9 reduce-scatter.2
  787.3 56.0 reduce-scatter.4
where the time goes:
time: 854 us; the launch traced here: 853 us
  waiting for transfers between devices  752 us (88%)
  starting transfers between devices  26 us (3%)
  local copies, waits for them, and re-layouts  23.2 us (3%)
  other arithmetic  21.3 us (2%)
  matrix products  16.5 us (2%)
  between operations  14 us (2%)
    psum x1, waiting for transfers between devices, body(): lax.psum(gated(second_section, lambda: contract_cols(grad_pre_b, up_full)...  153 us
    psum x1, waiting for transfers between devices, body(): out_sum = lax.psum(out_part.astype(jnp.bfloat16), 'col').astype(jnp.float32)  148 us
    ppermute x2, waiting for transfers between devices, from_behind(): return lax.ppermute(value, axis, pairs)  105 us
    all_gather x1, waiting for transfers between devices, body(): whole_tokens = lax.all_gather(tokens, 'col', axis=0, tiled=True)  80.5 us
    reduce_scatter x1, waiting for transfers between devices, body(): lax.psum_scatter(down_term.astype(jnp.bfloat16), 'row', scatter_dimension...  55.6 us
    psum x1, waiting for transfers between devices, body(): pre_a = lax.psum(pre_part.astype(jnp.bfloat16), 'row').astype(jnp.float32)  51.9 us
    reduce_scatter x1, waiting for transfers between devices, body(): lax.psum_scatter(up_term.astype(jnp.bfloat16), 'row', scatter_dimension=0...  50.6 us
    all_to_all x1, waiting for transfers between devices, body(): lax.all_to_all(boundary_feat, 'row', split_axis=0, concat_axis=1, tiled=T...  48.9 us
  transfers between devices with their start and end apart: 13, of which 11 were waited for; matrix products, arithmetic and copies ran while one was open for 4% of the time, Pallas kernels for 0%

commit v1 on v0

v1 whole, which is shorter than its diff:
```python
import jax
import jax.numpy as jnp
from jax import lax
from jax.sharding import PartitionSpec as P

NY = 4
NZ = 8
Z_NEAR = 1
Z_FAR = (2, 4, 6)
Y_STEPS = (1, 2, 3)


def gelu(values):
    return jax.nn.gelu(values, approximate=True)


def gelu_grad(values, upstream):
    return jax.vjp(gelu, values)[1](upstream)[0]


def swap_col(value, dz, dy):
    pairs = []
    for z in range(NZ):
        for y in range(NY):
            pairs.append((z * NY + y, (z ^ dz) * NY + (y ^ dy)))
    return lax.ppermute(value, "col", pairs)


def swap_section(value, dz):
    cols = NZ * NY
    pairs = []
    for s in range(2):
        for z in range(NZ):
            for y in range(NY):
                pairs.append((s * cols + z * NY + y, (1 - s) * cols + (z ^ dz) * NY + y))
    return lax.ppermute(value, ("section", "col"), pairs)


def swap_row(value, by):
    return lax.ppermute(value, "row", [(r, r ^ by) for r in range(4)])


def dot(left, right, dims):
    return lax.dot_general(left, right, (dims, ((), ())), preferred_element_type=jnp.float32)


def bf16(values):
    return values.astype(jnp.bfloat16)


def f32(values):
    return values.astype(jnp.float32)


def gather_z(shard):
    near = jnp.concatenate([shard] + [swap_col(shard, k, 0) for k in Z_FAR], 0)
    return jnp.concatenate([near, swap_col(near, Z_NEAR, 0)], 0)


def gather_y(block):
    return [block] + [swap_col(block, 0, k) for k in Y_STEPS]


def scatter_z_across(partial):
    half = partial.shape[0] // 2
    kept = bf16(f32(partial[:half]) + f32(swap_col(partial[half:], Z_NEAR, 0)))
    rows = half // 4
    total = f32(swap_section(kept[:rows], 0))
    for i, k in enumerate(Z_FAR):
        total = total + f32(swap_section(kept[(i + 1) * rows : (i + 2) * rows], k))
    return total


def reduce_row(partial, core):
    blocks, tokens, width = partial.shape
    halves = partial.reshape(blocks, 2, tokens // 2, width)
    mine = lax.dynamic_index_in_dim(halves, core, 1, False)
    other = lax.dynamic_index_in_dim(halves, 1 - core, 1, False)
    chip = f32(mine) + f32(swap_row(other, 1))
    return chip + f32(swap_row(bf16(chip), 2))


def join_cores(mine, core, axis):
    other = swap_row(mine, 1)
    first = jnp.where(core == 0, mine, other)
    second = jnp.where(core == 0, other, mine)
    return jnp.concatenate([first, second], axis)


def body(tokens, w_up, w_down, cotangent):
    first_section = lax.axis_index("section") == 0
    row = lax.axis_index("row")
    core = row % 2
    col = lax.axis_index("col")
    z = col // NY
    y = col % NY
    shard, width = tokens.shape
    up = w_up[0]
    down = w_down[0].T
    w_one = jnp.where(first_section, up, down)
    w_two = jnp.where(first_section, down, up)
    hidden_width = up.shape[1]

    rows = cotangent.shape[0] // (shard * NY)
    mine = lax.dynamic_index_in_dim(cotangent.reshape(rows, NY, shard, -1), y, 1, False)
    spread = lax.all_to_all(mine, "row", split_axis=2, concat_axis=0, tiled=True)
    order = [0, *Z_FAR]
    order = order + [k ^ Z_NEAR for k in order]
    cot = jnp.concatenate(
        [lax.dynamic_index_in_dim(spread, z ^ k, 0, False) for k in order], 0
    )

    ones = gather_y(w_one)
    x_a = gather_z(tokens)
    start = jnp.where(first_section, x_a, cot)
    part = jnp.stack([bf16(dot(start, w, ((1,), (0,)))) for w in ones], 0)
    sum_one = reduce_row(part, core)
    hidden_a = bf16(gelu(sum_one))
    twos = jnp.stack(gather_y(w_two), 0)

    def leave(acts):
        return bf16(dot(acts, twos, ((0, 2), (0, 2))))

    def enter(acts):
        return jnp.stack([bf16(dot(acts, twos[k], ((1,), (0,)))) for k in range(NY)], 0)

    out = scatter_z_across(leave(join_cores(hidden_a, core, 1)))
    x_b = gather_z(bf16(f32(tokens) + out))
    pre_b = reduce_row(enter(x_b), core)
    hidden_b = bf16(gelu(pre_b))
    grad_pre_b = bf16(gelu_grad(pre_b, sum_one))
    back = scatter_z_across(leave(join_cores(grad_pre_b, core, 1)))
    grad_a = gather_z(bf16(f32(cot[:shard]) + back))
    grad_hidden_a = reduce_row(enter(grad_a), core)
    grad_pre_a = bf16(gelu_grad(sum_one, grad_hidden_a))

    hidden = jnp.where(first_section, hidden_a, hidden_b)
    grad_pre = jnp.where(first_section, grad_pre_a, grad_pre_b)
    x = jnp.where(first_section, x_a, x_b)
    grad = jnp.where(first_section, grad_a, cot)

    def own_hidden(acts):
        pieces = [acts[0]] + [swap_col(acts[k], 0, k) for k in Y_STEPS]
        joined = join_cores(jnp.stack(pieces, 0), core, 1)
        return joined.reshape(-1, hidden_width)

    x_all = jnp.concatenate(gather_y(x), 0)
    grad_all = jnp.concatenate(gather_y(grad), 0)
    grad_down = dot(own_hidden(hidden), grad_all, ((0,), (0,)))
    grad_up = dot(x_all, own_hidden(grad_pre), ((0,), (0,)))
    return (grad_up[None], grad_down[None])


def solution(mesh):
    placed = (
        P("col", "row"),
        P("section", "row", "col"),
        P("section", "col", "row"),
        P("row", None),
    )
    return jax.shard_map(
        body,
        mesh=mesh,
        in_specs=placed,
        out_specs=(P("section", "row", "col"), P("section", "col", "row")),
        check_vma=False,
    )
```

time: 854 us -> 349 us (0.41)
  waiting for transfers between devices: 752 us -> 159 us
  starting transfers between devices: 26 us -> 103 us
  between operations: 14 us -> 1.39 us
  local copies, waits for them, and re-layouts: 23.2 us -> 34.7 us
  matrix products: 16.5 us -> 27.8 us
    psum x4 -> x0, waiting for transfers between devices: 383 us -> none  [the longest x1 153 us: body(): lax.psum(gated(second_section, lambda: contract_cols(grad_pre_b, up_full)...]
    reduce_scatter x2 -> x0, waiting for transfers between devices: 106 us -> none  [the longest x1 55.6 us: body(): lax.psum_scatter(down_term.astype(jnp.bfloat16), 'row', scatter_dimension...]
    ppermute x2 -> x50, starting transfers between devices: 4.52 us -> 96.7 us  [the longest x32 59.3 us: swap_col(): return lax.ppermute(value, 'col', pairs)]
    all_gather x3 -> x0, waiting for transfers between devices: 80.5 us -> none  [the longest x1 80.5 us: body(): whole_tokens = lax.all_gather(tokens, 'col', axis=0, tiled=True)]
    all_to_all x2 -> x1, waiting for transfers between devices: 75.4 us -> 0.22 us  [body(): lax.all_to_all(mine, 'row', split_axis=2, concat_axis=0, tiled=True)]
    ppermute x2 -> x50, waiting for transfers between devices: 105 us -> 158 us  [the longest x32 112 us: swap_col(): return lax.ppermute(value, 'col', pairs)]
    unnamed x20 -> x38, local copies, waits for them, and re-layouts: 6.09 us -> 24.8 us
    all_to_all x2 -> x1, starting transfers between devices: 21.2 us -> 6.09 us  [body(): lax.all_to_all(mine, 'row', split_axis=2, concat_axis=0, tiled=True)]
  transfers between devices with their start and end apart: 13 -> 51, of which waited for: 11 -> 29; matrix products, arithmetic and copies ran while one was open for 4% -> 15% of each run, Pallas kernels for 0% -> 0%
where the time goes in v1:
time: 349 us; the launch traced here: 343 us
  waiting for transfers between devices  159 us (46%)
  starting transfers between devices  103 us (30%)
  local copies, waits for them, and re-layouts  34.7 us (10%)
  matrix products  27.8 us (8%)
  other arithmetic  18.1 us (5%)
    ppermute x32, waiting for transfers between devices, swap_col(): return lax.ppermute(value, 'col', pairs)  112 us
    ppermute x32, starting transfers between devices, swap_col(): return lax.ppermute(value, 'col', pairs)  59.3 us
    ppermute x10, waiting for transfers between devices, swap_row(): return lax.ppermute(value, 'row', [(r, r ^ by) for r in range(4)])  32.7 us
    dot_general x16, matrix products, dot(): lax.dot_general(left, right, (dims, ((), ())), preferred_element_type=jnp...  27.8 us
    unnamed x38, local copies, waits for them, and re-layouts  24.8 us
    ppermute x10, starting transfers between devices, swap_row(): return lax.ppermute(value, 'row', [(r, r ^ by) for r in range(4)])  21.7 us
    ppermute x8, starting transfers between devices, swap_section(): return lax.ppermute(value, ('section', 'col'), pairs)  15.6 us
    ppermute x8, waiting for transfers between devices, swap_section(): return lax.ppermute(value, ('section', 'col'), pairs)  13.5 us
  transfers between devices with their start and end apart: 51, of which 29 were waited for; matrix products, arithmetic and copies ran while one was open for 15% of the time, Pallas kernels for 0%

profile of v1, /device:TPU:1, one launch (start us, length us, event | category | flops | bytes accessed | tf_op | source)
XLA Modules:
  0.0 343.2 jit_solution(13992255831470045082)
XLA Ops:
  0.6 6.9 %collective-permute-start.2 = (bf16[32,1024]{1,0:T(8,128)(2,1)}, bf16[32,1024]{1,0:T(8,128)(2,1)S(1)}, u32[]{:S(2)}, u32[]{:S(2)}) collective-permute-start(bf16[32,1024]{1,0:T(8,128)(2,1)} %param.4), channel_id=1, source_target_pairs={{0,24},{1,25},{2,26},{3,27},{4,28},{5,29},{6,30},{7,31},{8,16},{9,... | collective-permute-start | bytes 196616 | tf_op jit(solution)/shard_map/ppermute | solution.py:26
  9.8 2.3 copy.25
  12.0 2.6 bitcast_select_fusion
  14.7 2.7 collective-permute-start.6
  18.6 5.3 %copy.31 = bf16[2,1,32,4096]{2,0,3,1:T(2,128)(2,1)} copy(bf16[2,1,32,4096]{3,2,1,0:T(8,128)(2,1)} %constant_dynamic-slice_fusion) | data formatting | bytes 1048576
  23.9 4.4 %bitcast_bitcast_fusion = bf16[4096,2,32]{2,1,0:T(2,128)(2,1)} fusion(bf16[2,1,32,4096]{2,0,3,1:T(2,128)(2,1)} %copy.31), kind=kLoop, calls=%fused_computation.139 | loop fusion | bytes 1048576
  28.3 4.5 %reshape.54 = bf16[4,2,32768]{2,1,0:T(2,128)(2,1)} reshape(bf16[4096,2,32]{2,1,0:T(2,128)(2,1)} %bitcast_bitcast_fusion) | data formatting | bytes 1048576
  32.9 6.1 %all-to-all-start = ((bf16[4,2,32768]{2,1,0:T(2,128)(2,1)}), bf16[4,2,32768]{2,1,0:T(2,128)(2,1)}, u32[]{:S(2)}, u32[]{:S(2)}) async-start(bf16[4,2,32768]{2,1,0:T(2,128)(2,1)} %reshape.54), calls=%async_computation | async-start | bytes 1048576 | tf_op jit(solution)/shard_map/all_to_all | solution.py:106
  42.5 5.1 %collective-permute-done.3 = bf16[128,1024]{1,0:T(8,128)(2,1)S(1)} collective-permute-done((bf16[128,1024]{1,0:T(8,128)(2,1)S(1)}, bf16[128,1024]{1,0:T(8,128)(2,1)S(1)}, u32[]{:S(2)}, u32[]{:S(2)}) %collective-permute-start.3) | collective-permute-done | bytes 262176 | tf_op jit(solution)/shard_map/ppermute | solution.py:26
  48.5 4.1 %reshape.55 = bf16[4096,2,32]{2,1,0:T(2,128)(2,1)} reshape(bf16[4,2,32768]{2,1,0:T(2,128)(2,1)} %all-to-all-done) | data formatting | bytes 1048576
  52.6 6.0 %copy.30 = bf16[2,32,4,1024]{3,2,1,0:T(4,128)(2,1)} copy(bf16[2,32,4,1024]{1,0,3,2:T(2,128)(2,1)} %bitcast.147) | data formatting | bytes 1048576 | tf_op jit(solution)/shard_map/all_to_all | solution.py:106
  65.8 1.7 convolution_convert_fusion.10
  68.4 1.7 collective-permute-start.7
  70.1 1.9 collective-permute-done.7
  73.2 2.8 collective-permute-start.8
  76.0 2.7 collective-permute-start.12
  79.3 8.7 %collective-permute-done.8 = bf16[4,128,512]{2,1,0:T(8,128)(2,1)S(1)} collective-permute-done((bf16[4,128,512]{2,1,0:T(8,128)(2,1)S(1)}, bf16[4,128,512]{2,1,0:T(8,128)(2,1)S(1)}, u32[]{:S(2)}, u32[]{:S(2)}) %collective-permute-start.8) | collective-permute-done | bytes 524320 | tf_op jit(solution)/shard_map/ppermute | solution.py:40
  88.8 2.3 multiply_convert_fusion.1
  92.5 1.9 collective-permute-done.9
  95.6 28.4 %collective-permute-done.12 = bf16[1024,512]{1,0:T(8,128)(2,1)} collective-permute-done((bf16[1024,512]{1,0:T(8,128)(2,1)}, bf16[1024,512]{1,0:T(8,128)(2,1)}, u32[]{:S(2)}, u32[]{:S(2)}) %collective-permute-start.12) | collective-permute-done | bytes 1048608 | tf_op jit(solution)/shard_map/ppermute | solution.py:26
  124.4 3.1 fusion.22
  128.4 5.3 %collective-permute-done.13 = bf16[128,1024]{1,0:T(8,128)(2,1)S(1)} collective-permute-done((bf16[128,1024]{1,0:T(8,128)(2,1)S(1)}, bf16[128,1024]{1,0:T(8,128)(2,1)S(1)}, u32[]{:S(2)}, u32[]{:S(2)}) %collective-permute-start.13) | collective-permute-done | bytes 262176 | tf_op jit(solution)/shard_map/ppermute | solution.py:26
  134.2 4.3 %collective-permute-start.17 = (bf16[32,1024]{1,0:T(8,128)(2,1)S(1)}, bf16[32,1024]{1,0:T(8,128)(2,1)S(1)}, u32[]{:S(2)}, u32[]{:S(2)}) collective-permute-start(bf16[32,1024]{1,0:T(8,128)(2,1)S(1)} %get-tuple-element.29), channel_id=1, source_target_pairs={{0,152},{1,153},{2,154},{3,155},{4,156},{5,157},{6,158},{7,159},{8... | collective-permute-start | bytes 196616 | tf_op jit(solution)/shard_map/ppermute | solution.py:36
  139.5 2.1 collective-permute-start.15
  141.6 5.4 %collective-permute-done.16 = bf16[32,1024]{1,0:T(8,128)(2,1)S(1)} collective-permute-done((bf16[32,1024]{1,0:T(8,128)(2,1)S(1)}, bf16[32,1024]{1,0:T(8,128)(2,1)S(1)}, u32[]{:S(2)}, u32[]{:S(2)}) %collective-permute-start.16) | collective-permute-done | bytes 65568 | tf_op jit(solution)/shard_map/ppermute | solution.py:36
  147.1 1.7 collective-permute-start.20
  148.8 2.3 collective-permute-start.19
  151.0 1.8 collective-permute-start.18
  152.8 3.0 collective-permute-done.19
  155.8 1.8 collective-permute-start.21
  157.7 5.8 %collective-permute-done.21 = bf16[128,1024]{1,0:T(8,128)(2,1)S(1)} collective-permute-done((bf16[128,1024]{1,0:T(8,128)(2,1)S(1)}, bf16[128,1024]{1,0:T(8,128)(2,1)S(1)}, u32[]{:S(2)}, u32[]{:S(2)}) %collective-permute-start.21) | collective-permute-done | bytes 262176 | tf_op jit(solution)/shard_map/ppermute | solution.py:26
  169.2 6.2 %collective-permute-start.25 = (bf16[4,128,512]{2,1,0:T(8,128)(2,1)S(1)}, bf16[4,128,512]{2,1,0:T(8,128)(2,1)S(1)}, u32[]{:S(2)}, u32[]{:S(2)}) collective-permute-start(bf16[4,128,512]{2,1,0:T(8,128)(2,1)S(1)} %dynamic-slice_bitcast_fusion.1), channel_id=1, source_target_pairs={{0,32},{32,0},{64,96},{96,64},{1,33},{33,1},{65,97},{97,65},{2,34}... | collective-permute-start | bytes 1572872 | tf_op jit(solution)/shard_map/ppermute | solution.py:40
  177.8 14.0 %collective-permute-done.26 = bf16[4,128,512]{2,1,0:T(8,128)(2,1)S(1)} collective-permute-done((bf16[4,128,512]{2,1,0:T(8,128)(2,1)S(1)}, bf16[4,128,512]{2,1,0:T(8,128)(2,1)S(1)}, u32[]{:S(2)}, u32[]{:S(2)}) %collective-permute-start.26) | collective-permute-done | bytes 524320 | tf_op jit(solution)/shard_map/ppermute | solution.py:40
  191.8 2.1 fusion.37
  196.8 3.1 fusion.23
  200.0 10.7 %collective-permute-start.28 = (bf16[128,1024]{1,0:T(8,128)(2,1)S(1)}, bf16[128,1024]{1,0:T(8,128)(2,1)S(1)}, u32[]{:S(2)}, u32[]{:S(2)}) collective-permute-start(bf16[128,1024]{1,0:T(8,128)(2,1)S(1)} %slice.87), channel_id=1, source_target_pairs={{0,4},{1,5},{2,6},{3,7},{4,0},{5,1},{6,2},{7,3},{8,12},{9,13},{10,... | collective-permute-start | bytes 786440 | tf_op jit(solution)/shard_map/ppermute | solution.py:26
  210.7 6.4 %collective-permute-done.28 = bf16[128,1024]{1,0:T(8,128)(2,1)S(1)} collective-permute-done((bf16[128,1024]{1,0:T(8,128)(2,1)S(1)}, bf16[128,1024]{1,0:T(8,128)(2,1)S(1)}, u32[]{:S(2)}, u32[]{:S(2)}) %collective-permute-start.28) | collective-permute-done | bytes 262176 | tf_op jit(solution)/shard_map/ppermute | solution.py:26
  218.0 2.2 collective-permute-start.32
  220.2 3.0 collective-permute-start.31
  223.2 1.8 collective-permute-start.30
  225.0 3.9 %collective-permute-done.31 = bf16[32,1024]{1,0:T(8,128)(2,1)S(1)} collective-permute-done((bf16[32,1024]{1,0:T(8,128)(2,1)S(1)}, bf16[32,1024]{1,0:T(8,128)(2,1)S(1)}, u32[]{:S(2)}, u32[]{:S(2)}) %collective-permute-start.31) | collective-permute-done | bytes 65568 | tf_op jit(solution)/shard_map/ppermute | solution.py:36
  229.0 4.1 %collective-permute-done.30 = bf16[32,1024]{1,0:T(8,128)(2,1)S(1)} collective-permute-done((bf16[32,1024]{1,0:T(8,128)(2,1)S(1)}, bf16[32,1024]{1,0:T(8,128)(2,1)S(1)}, u32[]{:S(2)}, u32[]{:S(2)}) %collective-permute-start.30) | collective-permute-done | bytes 65568 | tf_op jit(solution)/shard_map/ppermute | solution.py:36
  234.0 2.3 collective-permute-start.34
  236.4 3.3 collective-permute-start.33
  242.4 4.4 %collective-permute-start.36 = (bf16[128,1024]{1,0:T(8,128)(2,1)S(1)}, bf16[128,1024]{1,0:T(8,128)(2,1)S(1)}, u32[]{:S(2)}, u32[]{:S(2)}) collective-permute-start(bf16[128,1024]{1,0:T(8,128)(2,1)S(1)} %pad_maximum_fusion.12), channel_id=1, source_target_pairs={{0,4},{1,5},{2,6},{3,7},{4,0},{5,1},{6,2},{7,3},{8,12},{9,13},{10,... | collective-permute-start | bytes 786440 | tf_op jit(solution)/shard_map/ppermute | solution.py:26
  246.8 6.2 %collective-permute-done.36 = bf16[128,1024]{1,0:T(8,128)(2,1)S(1)} collective-permute-done((bf16[128,1024]{1,0:T(8,128)(2,1)S(1)}, bf16[128,1024]{1,0:T(8,128)(2,1)S(1)}, u32[]{:S(2)}, u32[]{:S(2)}) %collective-permute-start.36) | collective-permute-done | bytes 262176 | tf_op jit(solution)/shard_map/ppermute | solution.py:26
  253.5 1.7 convolution_convert_fusion
  255.2 1.7 convolution_convert_fusion.1
  256.9 1.7 convolution_convert_fusion.2
  262.4 2.0 collective-permute-start.45
  268.3 1.8 collective-permute-done.44
  271.4 1.9 collective-permute-start.46
  273.3 3.2 collective-permute-done.38
  276.5 2.1 broadcast_select_fusion
  278.6 2.3 collective-permute-start.41
  281.8 2.8 collective-permute-start.47
  285.7 23.2 %collective-permute-done.40 = bf16[128,512]{1,0:T(8,128)(2,1)S(1)} collective-permute-done((bf16[128,512]{1,0:T(8,128)(2,1)S(1)}, bf16[128,512]{1,0:T(8,128)(2,1)S(1)}, u32[]{:S(2)}, u32[]{:S(2)}) %collective-permute-start.40) | collective-permute-done | bytes 131104 | tf_op jit(solution)/shard_map/ppermute | solution.py:26
  308.9 2.2 collective-permute-start.24
  311.9 3.9 %collective-permute-start.42 = (bf16[4,128,512]{2,1,0:T(8,128)(2,1)S(1)}, bf16[4,128,512]{2,1,0:T(8,128)(2,1)S(1)}, u32[]{:S(2)}, u32[]{:S(2)}) collective-permute-start(bf16[4,128,512]{2,1,0:T(8,128)(2,1)S(1)} %pad_maximum_fusion.8), channel_id=1, source_target_pairs={{0,32},{32,0},{64,96},{96,64},{1,33},{33,1},{65,97},{97,65},{2,34}... | collective-permute-start | bytes 1572872 | tf_op jit(solution)/shard_map/ppermute | solution.py:40
  317.0 2.6 fusion.16
  319.8 9.4 %collective-permute-done.24 = bf16[256,1024]{1,0:T(8,128)(2,1)S(1)} collective-permute-done((bf16[256,1024]{1,0:T(8,128)(2,1)S(1)}, bf16[256,1024]{1,0:T(8,128)(2,1)S(1)}, u32[]{:S(2)}, u32[]{:S(2)}) %collective-permute-start.24) | collective-permute-done | bytes 524320 | tf_op jit(solution)/shard_map/ppermute | solution.py:26
  329.1 1.9 collective-permute-done.23
  331.0 9.3 %collective-permute-done.22 = bf16[256,1024]{1,0:T(8,128)(2,1)S(1)} collective-permute-done((bf16[256,1024]{1,0:T(8,128)(2,1)S(1)}, bf16[256,1024]{1,0:T(8,128)(2,1)S(1)}, u32[]{:S(2)}, u32[]{:S(2)}) %collective-permute-start.22) | collective-permute-done | bytes 524320 | tf_op jit(solution)/shard_map/ppermute | solution.py:26
  340.3 2.6 fusion.19
  (137 shorter events, 53.0 us)
Async XLA Ops:
  0.6 17.1 %copy-start = (bf16[256,4096]{1,0:T(8,128)(2,1)S(1)}, bf16[256,4096]{1,0:T(8,128)(2,1)}, u32[]{:S(2)}) copy-start(bf16[256,4096]{1,0:T(8,128)(2,1)} %param.7) | copy-start | bytes 6291460
  0.6 38.9 %collective-permute-start.2 = (bf16[32,1024]{1,0:T(8,128)(2,1)}, bf16[32,1024]{1,0:T(8,128)(2,1)S(1)}, u32[]{:S(2)}, u32[]{:S(2)}) collective-permute-start(bf16[32,1024]{1,0:T(8,128)(2,1)} %param.4), channel_id=1, source_target_pairs={{0,24},{1,25},{2,26},{3,27},{4,28},{5,29},{6,30},{7,31},{8,16},{9,... | collective-permute-start | bytes 196616 | tf_op jit(solution)/shard_map/ppermute | solution.py:26
  7.6 32.2 %collective-permute-start.1 = (bf16[32,1024]{1,0:T(8,128)(2,1)}, bf16[32,1024]{1,0:T(8,128)(2,1)S(1)}, u32[]{:S(2)}, u32[]{:S(2)}) collective-permute-start(bf16[32,1024]{1,0:T(8,128)(2,1)} %param.4), channel_id=1, source_target_pairs={{0,16},{1,17},{2,18},{3,19},{4,20},{5,21},{6,22},{7,23},{8,24},{9,... | collective-permute-start | bytes 196616 | tf_op jit(solution)/shard_map/ppermute | solution.py:26
  8.6 31.2 %collective-permute-start = (bf16[32,1024]{1,0:T(8,128)(2,1)}, bf16[32,1024]{1,0:T(8,128)(2,1)S(1)}, u32[]{:S(2)}, u32[]{:S(2)}) collective-permute-start(bf16[32,1024]{1,0:T(8,128)(2,1)} %param.4), channel_id=1, source_target_pairs={{0,8},{1,9},{2,10},{3,11},{4,12},{5,13},{6,14},{7,15},{8,0},{9,1},... | collective-permute-start | bytes 196616 | tf_op jit(solution)/shard_map/ppermute | solution.py:26
  14.7 47.7 %collective-permute-start.6 = (bf16[1024,512]{1,0:T(8,128)(2,1)S(1)}, bf16[1024,512]{1,0:T(8,128)(2,1)}, u32[]{:S(2)}, u32[]{:S(2)}) collective-permute-start(bf16[1024,512]{1,0:T(8,128)(2,1)S(1)} %get-tuple-element.7), channel_id=1, source_target_pairs={{0,3},{1,2},{2,1},{3,0},{4,7},{5,6},{6,5},{7,4},{8,11},{9,10},{10,... | collective-permute-start | bytes 3145736 | tf_op jit(solution)/shard_map/ppermute | solution.py:26
  17.4 46.7 %collective-permute-start.5 = (bf16[1024,512]{1,0:T(8,128)(2,1)S(1)}, bf16[1024,512]{1,0:T(8,128)(2,1)}, u32[]{:S(2)}, u32[]{:S(2)}) collective-permute-start(bf16[1024,512]{1,0:T(8,128)(2,1)S(1)} %get-tuple-element.7), channel_id=1, source_target_pairs={{0,2},{1,3},{2,0},{3,1},{4,6},{5,7},{6,4},{7,5},{8,10},{9,11},{10,... | collective-permute-start | bytes 3145736 | tf_op jit(solution)/shard_map/ppermute | solution.py:26
  28.3 10.6 %copy-start.7 = (bf16[32,1024]{1,0:T(8,128)(2,1)S(1)}, bf16[32,1024]{1,0:T(8,128)(2,1)}, u32[]{:S(2)}) copy-start(bf16[32,1024]{1,0:T(8,128)(2,1)} %param.4) | copy-start | bytes 196612
  32.9 15.7 %all-to-all-start = ((bf16[4,2,32768]{2,1,0:T(2,128)(2,1)}), bf16[4,2,32768]{2,1,0:T(2,128)(2,1)}, u32[]{:S(2)}, u32[]{:S(2)}) async-start(bf16[4,2,32768]{2,1,0:T(2,128)(2,1)} %reshape.54), calls=%async_computation | async-start | bytes 1048576 | tf_op jit(solution)/shard_map/all_to_all | solution.py:106
  39.6 26.2 %collective-permute-start.4 = (bf16[1024,512]{1,0:T(8,128)(2,1)S(1)}, bf16[1024,512]{1,0:T(8,128)(2,1)}, u32[]{:S(2)}, u32[]{:S(2)}) collective-permute-start(bf16[1024,512]{1,0:T(8,128)(2,1)S(1)} %get-tuple-element.7), channel_id=1, source_target_pairs={{0,1},{1,0},{2,3},{3,2},{4,5},{5,4},{6,7},{7,6},{8,9},{9,8},{10,11... | collective-permute-start | bytes 3145736 | tf_op jit(solution)/shard_map/ppermute | solution.py:26
  39.8 7.8 %collective-permute-start.3 = (bf16[128,1024]{1,0:T(8,128)(2,1)S(1)}, bf16[128,1024]{1,0:T(8,128)(2,1)S(1)}, u32[]{:S(2)}, u32[]{:S(2)}) collective-permute-start(bf16[128,1024]{1,0:T(8,128)(2,1)S(1)} %pad_maximum_fusion.10), channel_id=1, source_target_pairs={{0,4},{1,5},{2,6},{3,7},{4,0},{5,1},{6,2},{7,3},{8,12},{9,13},{10,... | collective-permute-start | bytes 786440 | tf_op jit(solution)/shard_map/ppermute | solution.py:26
  59.8 0.8 copy-start.4
  60.7 3.4 copy-start.5
  68.4 3.6 %collective-permute-start.7 = (bf16[4,128,512]{2,1,0:T(8,128)(2,1)}, bf16[4,128,512]{2,1,0:T(8,128)(2,1)}, u32[]{:S(2)}, u32[]{:S(2)}) collective-permute-start(bf16[4,128,512]{2,1,0:T(8,128)(2,1)} %dynamic-slice_bitcast_fusion.2), channel_id=1, source_target_pairs={{0,32},{32,0},{64,96},{96,64},{1,33},{33,1},{65,97},{97,65},{2,34}... | collective-permute-start | bytes 1572872 | tf_op jit(solution)/shard_map/ppermute | solution.py:40
  73.2 14.8 %collective-permute-start.8 = (bf16[4,128,512]{2,1,0:T(8,128)(2,1)S(1)}, bf16[4,128,512]{2,1,0:T(8,128)(2,1)S(1)}, u32[]{:S(2)}, u32[]{:S(2)}) collective-permute-start(bf16[4,128,512]{2,1,0:T(8,128)(2,1)S(1)} %fusion.44), channel_id=1, source_target_pairs={{0,64},{32,96},{64,0},{96,32},{1,65},{33,97},{65,1},{97,33},{2,66}... | collective-permute-start | bytes 1572872 | tf_op jit(solution)/shard_map/ppermute | solution.py:40
  76.0 48.0 %collective-permute-start.12 = (bf16[1024,512]{1,0:T(8,128)(2,1)}, bf16[1024,512]{1,0:T(8,128)(2,1)}, u32[]{:S(2)}, u32[]{:S(2)}) collective-permute-start(bf16[1024,512]{1,0:T(8,128)(2,1)} %get-tuple-element.6), channel_id=1, source_target_pairs={{0,3},{1,2},{2,1},{3,0},{4,7},{5,6},{6,5},{7,4},{8,11},{9,10},{10,... | collective-permute-start | bytes 3145736 | tf_op jit(solution)/shard_map/ppermute | solution.py:26
  78.7 45.4 %collective-permute-start.11 = (bf16[1024,512]{1,0:T(8,128)(2,1)}, bf16[1024,512]{1,0:T(8,128)(2,1)}, u32[]{:S(2)}, u32[]{:S(2)}) collective-permute-start(bf16[1024,512]{1,0:T(8,128)(2,1)} %get-tuple-element.6), channel_id=1, source_target_pairs={{0,2},{1,3},{2,0},{3,1},{4,6},{5,7},{6,4},{7,5},{8,10},{9,11},{10,... | collective-permute-start | bytes 3145736 | tf_op jit(solution)/shard_map/ppermute | solution.py:26
  78.7 45.7 %collective-permute-start.10 = (bf16[1024,512]{1,0:T(8,128)(2,1)}, bf16[1024,512]{1,0:T(8,128)(2,1)}, u32[]{:S(2)}, u32[]{:S(2)}) collective-permute-start(bf16[1024,512]{1,0:T(8,128)(2,1)} %get-tuple-element.6), channel_id=1, source_target_pairs={{0,1},{1,0},{2,3},{3,2},{4,5},{5,4},{6,7},{7,6},{8,9},{9,8},{10,11... | collective-permute-start | bytes 3145736 | tf_op jit(solution)/shard_map/ppermute | solution.py:26
  88.0 0.8 copy-start.2
  91.2 3.2 collective-permute-start.9
  92.5 31.9 %copy-start.1 = (bf16[1024,512]{1,0:T(8,128)(2,1)S(1)}, bf16[1024,512]{1,0:T(8,128)(2,1)}, u32[]{:S(2)}) copy-start(bf16[1024,512]{1,0:T(8,128)(2,1)} %get-tuple-element.6) | copy-start | bytes 3145732
  127.6 6.1 %collective-permute-start.13 = (bf16[128,1024]{1,0:T(8,128)(2,1)S(1)}, bf16[128,1024]{1,0:T(8,128)(2,1)S(1)}, u32[]{:S(2)}, u32[]{:S(2)}) collective-permute-start(bf16[128,1024]{1,0:T(8,128)(2,1)S(1)} %slice.81), channel_id=1, source_target_pairs={{0,4},{1,5},{2,6},{3,7},{4,0},{5,1},{6,2},{7,3},{8,12},{9,13},{10,... | collective-permute-start | bytes 786440 | tf_op jit(solution)/shard_map/ppermute | solution.py:26
  133.8 7.8 %collective-permute-start.14 = (bf16[32,1024]{1,0:T(8,128)(2,1)S(1)}, bf16[32,1024]{1,0:T(8,128)(2,1)S(1)}, u32[]{:S(2)}, u32[]{:S(2)}) collective-permute-start(bf16[32,1024]{1,0:T(8,128)(2,1)S(1)} %get-tuple-element.28), channel_id=1, source_target_pairs={{0,128},{1,129},{2,130},{3,131},{4,132},{5,133},{6,134},{7,135},{8... | collective-permute-start | bytes 196616 | tf_op jit(solution)/shard_map/ppermute | solution.py:36
  134.2 7.4 %collective-permute-start.17 = (bf16[32,1024]{1,0:T(8,128)(2,1)S(1)}, bf16[32,1024]{1,0:T(8,128)(2,1)S(1)}, u32[]{:S(2)}, u32[]{:S(2)}) collective-permute-start(bf16[32,1024]{1,0:T(8,128)(2,1)S(1)} %get-tuple-element.29), channel_id=1, source_target_pairs={{0,152},{1,153},{2,154},{3,155},{4,156},{5,157},{6,158},{7,159},{8... | collective-permute-start | bytes 196616 | tf_op jit(solution)/shard_map/ppermute | solution.py:36
  138.5 8.5 %collective-permute-start.16 = (bf16[32,1024]{1,0:T(8,128)(2,1)S(1)}, bf16[32,1024]{1,0:T(8,128)(2,1)S(1)}, u32[]{:S(2)}, u32[]{:S(2)}) collective-permute-start(bf16[32,1024]{1,0:T(8,128)(2,1)S(1)} %get-tuple-element.30), channel_id=1, source_target_pairs={{0,144},{1,145},{2,146},{3,147},{4,148},{5,149},{6,150},{7,151},{8... | collective-permute-start | bytes 196616 | tf_op jit(solution)/shard_map/ppermute | solution.py:36
  139.5 7.5 %collective-permute-start.15 = (bf16[32,1024]{1,0:T(8,128)(2,1)S(1)}, bf16[32,1024]{1,0:T(8,128)(2,1)S(1)}, u32[]{:S(2)}, u32[]{:S(2)}) collective-permute-start(bf16[32,1024]{1,0:T(8,128)(2,1)S(1)} %get-tuple-element.31), channel_id=1, source_target_pairs={{0,136},{1,137},{2,138},{3,139},{4,140},{5,141},{6,142},{7,143},{8... | collective-permute-start | bytes 196616 | tf_op jit(solution)/shard_map/ppermute | solution.py:36
  147.1 5.7 %collective-permute-start.20 = (bf16[32,1024]{1,0:T(8,128)(2,1)S(1)}, bf16[32,1024]{1,0:T(8,128)(2,1)S(1)}, u32[]{:S(2)}, u32[]{:S(2)}) collective-permute-start(bf16[32,1024]{1,0:T(8,128)(2,1)S(1)} %get-tuple-element.5), channel_id=1, source_target_pairs={{0,24},{1,25},{2,26},{3,27},{4,28},{5,29},{6,30},{7,31},{8,16},{9,... | collective-permute-start | bytes 196616 | tf_op jit(solution)/shard_map/ppermute | solution.py:26
  148.8 7.0 %collective-permute-start.19 = (bf16[32,1024]{1,0:T(8,128)(2,1)S(1)}, bf16[32,1024]{1,0:T(8,128)(2,1)S(1)}, u32[]{:S(2)}, u32[]{:S(2)}) collective-permute-start(bf16[32,1024]{1,0:T(8,128)(2,1)S(1)} %get-tuple-element.5), channel_id=1, source_target_pairs={{0,16},{1,17},{2,18},{3,19},{4,20},{5,21},{6,22},{7,23},{8,24},{9,... | collective-permute-start | bytes 196616 | tf_op jit(solution)/shard_map/ppermute | solution.py:26
  151.0 4.8 %collective-permute-start.18 = (bf16[32,1024]{1,0:T(8,128)(2,1)S(1)}, bf16[32,1024]{1,0:T(8,128)(2,1)S(1)}, u32[]{:S(2)}, u32[]{:S(2)}) collective-permute-start(bf16[32,1024]{1,0:T(8,128)(2,1)S(1)} %get-tuple-element.5), channel_id=1, source_target_pairs={{0,8},{1,9},{2,10},{3,11},{4,12},{5,13},{6,14},{7,15},{8,0},{9,1},... | collective-permute-start | bytes 196616 | tf_op jit(solution)/shard_map/ppermute | solution.py:26
  155.8 7.7 %collective-permute-start.21 = (bf16[128,1024]{1,0:T(8,128)(2,1)S(1)}, bf16[128,1024]{1,0:T(8,128)(2,1)S(1)}, u32[]{:S(2)}, u32[]{:S(2)}) collective-permute-start(bf16[128,1024]{1,0:T(8,128)(2,1)S(1)} %pad_maximum_fusion.11), channel_id=1, source_target_pairs={{0,4},{1,5},{2,6},{3,7},{4,0},{5,1},{6,2},{7,3},{8,12},{9,13},{10,... | collective-permute-start | bytes 786440 | tf_op jit(solution)/shard_map/ppermute | solution.py:26
  169.0 22.8 %copy-start.3 = (bf16[4,128,512]{2,1,0:T(8,128)(2,1)S(1)}, bf16[4,128,512]{2,1,0:T(8,128)(2,1)}, u32[]{:S(2)}) copy-start(bf16[4,128,512]{2,1,0:T(8,128)(2,1)} %copy-done.2) | copy-start | bytes 1572868
  169.2 7.8 %collective-permute-start.25 = (bf16[4,128,512]{2,1,0:T(8,128)(2,1)S(1)}, bf16[4,128,512]{2,1,0:T(8,128)(2,1)S(1)}, u32[]{:S(2)}, u32[]{:S(2)}) collective-permute-start(bf16[4,128,512]{2,1,0:T(8,128)(2,1)S(1)} %dynamic-slice_bitcast_fusion.1), channel_id=1, source_target_pairs={{0,32},{32,0},{64,96},{96,64},{1,33},{33,1},{65,97},{97,65},{2,34}... | collective-permute-start | bytes 1572872 | tf_op jit(solution)/shard_map/ppermute | solution.py:40
  177.1 14.7 %collective-permute-start.26 = (bf16[4,128,512]{2,1,0:T(8,128)(2,1)S(1)}, bf16[4,128,512]{2,1,0:T(8,128)(2,1)S(1)}, u32[]{:S(2)}, u32[]{:S(2)}) collective-permute-start(bf16[4,128,512]{2,1,0:T(8,128)(2,1)S(1)} %fusion.45), channel_id=1, source_target_pairs={{0,64},{32,96},{64,0},{96,32},{1,65},{33,97},{65,1},{97,33},{2,66}... | collective-permute-start | bytes 1572872 | tf_op jit(solution)/shard_map/ppermute | solution.py:40
  193.9 2.8 collective-permute-start.27
  200.0 17.1 %collective-permute-start.28 = (bf16[128,1024]{1,0:T(8,128)(2,1)S(1)}, bf16[128,1024]{1,0:T(8,128)(2,1)S(1)}, u32[]{:S(2)}, u32[]{:S(2)}) collective-permute-start(bf16[128,1024]{1,0:T(8,128)(2,1)S(1)} %slice.87), channel_id=1, source_target_pairs={{0,4},{1,5},{2,6},{3,7},{4,0},{5,1},{6,2},{7,3},{8,12},{9,13},{10,... | collective-permute-start | bytes 786440 | tf_op jit(solution)/shard_map/ppermute | solution.py:26
  217.2 7.8 %collective-permute-start.29 = (bf16[32,1024]{1,0:T(8,128)(2,1)S(1)}, bf16[32,1024]{1,0:T(8,128)(2,1)S(1)}, u32[]{:S(2)}, u32[]{:S(2)}) collective-permute-start(bf16[32,1024]{1,0:T(8,128)(2,1)S(1)} %get-tuple-element.24), channel_id=1, source_target_pairs={{0,128},{1,129},{2,130},{3,131},{4,132},{5,133},{6,134},{7,135},{8... | collective-permute-start | bytes 196616 | tf_op jit(solution)/shard_map/ppermute | solution.py:36
  218.0 7.0 %collective-permute-start.32 = (bf16[32,1024]{1,0:T(8,128)(2,1)S(1)}, bf16[32,1024]{1,0:T(8,128)(2,1)S(1)}, u32[]{:S(2)}, u32[]{:S(2)}) collective-permute-start(bf16[32,1024]{1,0:T(8,128)(2,1)S(1)} %get-tuple-element.25), channel_id=1, source_target_pairs={{0,152},{1,153},{2,154},{3,155},{4,156},{5,157},{6,158},{7,159},{8... | collective-permute-start | bytes 196616 | tf_op jit(solution)/shard_map/ppermute | solution.py:36
  220.2 8.7 %collective-permute-start.31 = (bf16[32,1024]{1,0:T(8,128)(2,1)S(1)}, bf16[32,1024]{1,0:T(8,128)(2,1)S(1)}, u32[]{:S(2)}, u32[]{:S(2)}) collective-permute-start(bf16[32,1024]{1,0:T(8,128)(2,1)S(1)} %get-tuple-element.26), channel_id=1, source_target_pairs={{0,144},{1,145},{2,146},{3,147},{4,148},{5,149},{6,150},{7,151},{8... | collective-permute-start | bytes 196616 | tf_op jit(solution)/shard_map/ppermute | solution.py:36
  223.2 9.8 %collective-permute-start.30 = (bf16[32,1024]{1,0:T(8,128)(2,1)S(1)}, bf16[32,1024]{1,0:T(8,128)(2,1)S(1)}, u32[]{:S(2)}, u32[]{:S(2)}) collective-permute-start(bf16[32,1024]{1,0:T(8,128)(2,1)S(1)} %get-tuple-element.27), channel_id=1, source_target_pairs={{0,136},{1,137},{2,138},{3,139},{4,140},{5,141},{6,142},{7,143},{8... | collective-permute-start | bytes 196616 | tf_op jit(solution)/shard_map/ppermute | solution.py:36
  233.9 5.7 %collective-permute-start.35 = (bf16[32,1024]{1,0:T(8,128)(2,1)S(1)}, bf16[32,1024]{1,0:T(8,128)(2,1)S(1)}, u32[]{:S(2)}, u32[]{:S(2)}) collective-permute-start(bf16[32,1024]{1,0:T(8,128)(2,1)S(1)} %get-tuple-element.3), channel_id=1, source_target_pairs={{0,24},{1,25},{2,26},{3,27},{4,28},{5,29},{6,30},{7,31},{8,16},{9,... | collective-permute-start | bytes 196616 | tf_op jit(solution)/shard_map/ppermute | solution.py:26
  234.0 7.1 %collective-permute-start.34 = (bf16[32,1024]{1,0:T(8,128)(2,1)S(1)}, bf16[32,1024]{1,0:T(8,128)(2,1)S(1)}, u32[]{:S(2)}, u32[]{:S(2)}) collective-permute-start(bf16[32,1024]{1,0:T(8,128)(2,1)S(1)} %get-tuple-element.3), channel_id=1, source_target_pairs={{0,16},{1,17},{2,18},{3,19},{4,20},{5,21},{6,22},{7,23},{8,24},{9,... | collective-permute-start | bytes 196616 | tf_op jit(solution)/shard_map/ppermute | solution.py:26
  236.4 6.0 %collective-permute-start.33 = (bf16[32,1024]{1,0:T(8,128)(2,1)S(1)}, bf16[32,1024]{1,0:T(8,128)(2,1)S(1)}, u32[]{:S(2)}, u32[]{:S(2)}) collective-permute-start(bf16[32,1024]{1,0:T(8,128)(2,1)S(1)} %get-tuple-element.3), channel_id=1, source_target_pairs={{0,8},{1,9},{2,10},{3,11},{4,12},{5,13},{6,14},{7,15},{8,0},{9,1},... | collective-permute-start | bytes 196616 | tf_op jit(solution)/shard_map/ppermute | solution.py:26
  242.4 10.7 %collective-permute-start.36 = (bf16[128,1024]{1,0:T(8,128)(2,1)S(1)}, bf16[128,1024]{1,0:T(8,128)(2,1)S(1)}, u32[]{:S(2)}, u32[]{:S(2)}) collective-permute-start(bf16[128,1024]{1,0:T(8,128)(2,1)S(1)} %pad_maximum_fusion.12), channel_id=1, source_target_pairs={{0,4},{1,5},{2,6},{3,7},{4,0},{5,1},{6,2},{7,3},{8,12},{9,13},{10,... | collective-permute-start | bytes 786440 | tf_op jit(solution)/shard_map/ppermute | solution.py:26
  258.8 2.7 collective-permute-start.37
  261.6 14.8 %collective-permute-start.38 = (bf16[4,128,512]{2,1,0:T(8,128)(2,1)S(1)}, bf16[4,128,512]{2,1,0:T(8,128)(2,1)S(1)}, u32[]{:S(2)}, u32[]{:S(2)}) collective-permute-start(bf16[4,128,512]{2,1,0:T(8,128)(2,1)S(1)} %fusion.46), channel_id=1, source_target_pairs={{0,64},{32,96},{64,0},{96,32},{1,65},{33,97},{65,1},{97,33},{2,66}... | collective-permute-start | bytes 1572872 | tf_op jit(solution)/shard_map/ppermute | solution.py:40
  262.4 6.0 %collective-permute-start.45 = (bf16[128,512]{1,0:T(8,128)(2,1)S(1)}, bf16[128,512]{1,0:T(8,128)(2,1)S(1)}, u32[]{:S(2)}, u32[]{:S(2)}) collective-permute-start(bf16[128,512]{1,0:T(8,128)(2,1)S(1)} %get-tuple-element.17), channel_id=1, source_target_pairs={{0,3},{1,2},{2,1},{3,0},{4,7},{5,6},{6,5},{7,4},{8,11},{9,10},{10,... | collective-permute-start | bytes 393224 | tf_op jit(solution)/shard_map/ppermute | solution.py:26
  264.4 5.8 %collective-permute-start.44 = (bf16[128,512]{1,0:T(8,128)(2,1)S(1)}, bf16[128,512]{1,0:T(8,128)(2,1)S(1)}, u32[]{:S(2)}, u32[]{:S(2)}) collective-permute-start(bf16[128,512]{1,0:T(8,128)(2,1)S(1)} %get-tuple-element.18), channel_id=1, source_target_pairs={{0,2},{1,3},{2,0},{3,1},{4,6},{5,7},{6,4},{7,5},{8,10},{9,11},{10,... | collective-permute-start | bytes 393224 | tf_op jit(solution)/shard_map/ppermute | solution.py:26
  264.9 6.4 %collective-permute-start.43 = (bf16[128,512]{1,0:T(8,128)(2,1)S(1)}, bf16[128,512]{1,0:T(8,128)(2,1)S(1)}, u32[]{:S(2)}, u32[]{:S(2)}) collective-permute-start(bf16[128,512]{1,0:T(8,128)(2,1)S(1)} %get-tuple-element.19), channel_id=1, source_target_pairs={{0,1},{1,0},{2,3},{3,2},{4,5},{5,4},{6,7},{7,6},{8,9},{9,8},{10,11... | collective-permute-start | bytes 393224 | tf_op jit(solution)/shard_map/ppermute | solution.py:26
  271.4 9.6 %copy-start.6 = (bf16[256,1024]{1,0:T(8,128)(2,1)S(1)}, bf16[256,1024]{1,0:T(8,128)(2,1)}, u32[]{:S(2)}) copy-start(bf16[256,1024]{1,0:T(8,128)(2,1)} %copy-done.5) | copy-start | bytes 1572868
  271.4 13.2 %collective-permute-start.46 = (bf16[4,128,512]{2,1,0:T(8,128)(2,1)S(1)}, bf16[4,128,512]{2,1,0:T(8,128)(2,1)S(1)}, u32[]{:S(2)}, u32[]{:S(2)}) collective-permute-start(bf16[4,128,512]{2,1,0:T(8,128)(2,1)S(1)} %pad_maximum_fusion.9), channel_id=1, source_target_pairs={{0,32},{32,0},{64,96},{96,64},{1,33},{33,1},{65,97},{97,65},{2,34}... | collective-permute-start | bytes 1572872 | tf_op jit(solution)/shard_map/ppermute | solution.py:40
  278.6 6.5 %collective-permute-start.41 = (bf16[128,512]{1,0:T(8,128)(2,1)S(1)}, bf16[128,512]{1,0:T(8,128)(2,1)S(1)}, u32[]{:S(2)}, u32[]{:S(2)}) collective-permute-start(bf16[128,512]{1,0:T(8,128)(2,1)S(1)} %get-tuple-element.21), channel_id=1, source_target_pairs={{0,3},{1,2},{2,1},{3,0},{4,7},{5,6},{6,5},{7,4},{8,11},{9,10},{10,... | collective-permute-start | bytes 393224 | tf_op jit(solution)/shard_map/ppermute | solution.py:26
  281.0 34.8 %collective-permute-start.49 = (bf16[256,1024]{1,0:T(8,128)(2,1)S(1)}, bf16[256,1024]{1,0:T(8,128)(2,1)S(1)}, u32[]{:S(2)}, u32[]{:S(2)}) collective-permute-start(bf16[256,1024]{1,0:T(8,128)(2,1)S(1)} %broadcast_select_fusion.9), channel_id=1, source_target_pairs={{0,3},{1,2},{2,1},{3,0},{4,7},{5,6},{6,5},{7,4},{8,11},{9,10},{10,... | collective-permute-start | bytes 1572872 | tf_op jit(solution)/shard_map/ppermute | solution.py:26
  281.8 34.2 %collective-permute-start.48 = (bf16[256,1024]{1,0:T(8,128)(2,1)S(1)}, bf16[256,1024]{1,0:T(8,128)(2,1)S(1)}, u32[]{:S(2)}, u32[]{:S(2)}) collective-permute-start(bf16[256,1024]{1,0:T(8,128)(2,1)S(1)} %broadcast_select_fusion.9), channel_id=1, source_target_pairs={{0,2},{1,3},{2,0},{3,1},{4,6},{5,7},{6,4},{7,5},{8,10},{9,11},{10,... | collective-permute-start | bytes 1572872 | tf_op jit(solution)/shard_map/ppermute | solution.py:26
  281.8 35.2 %collective-permute-start.47 = (bf16[256,1024]{1,0:T(8,128)(2,1)S(1)}, bf16[256,1024]{1,0:T(8,128)(2,1)S(1)}, u32[]{:S(2)}, u32[]{:S(2)}) collective-permute-start(bf16[256,1024]{1,0:T(8,128)(2,1)S(1)} %broadcast_select_fusion.9), channel_id=1, source_target_pairs={{0,1},{1,0},{2,3},{3,2},{4,5},{5,4},{6,7},{7,6},{8,9},{9,8},{10,11... | collective-permute-start | bytes 1572872 | tf_op jit(solution)/shard_map/ppermute | solution.py:26
  284.6 24.3 %collective-permute-start.40 = (bf16[128,512]{1,0:T(8,128)(2,1)S(1)}, bf16[128,512]{1,0:T(8,128)(2,1)S(1)}, u32[]{:S(2)}, u32[]{:S(2)}) collective-permute-start(bf16[128,512]{1,0:T(8,128)(2,1)S(1)} %get-tuple-element.22), channel_id=1, source_target_pairs={{0,2},{1,3},{2,0},{3,1},{4,6},{5,7},{6,4},{7,5},{8,10},{9,11},{10,... | collective-permute-start | bytes 393224 | tf_op jit(solution)/shard_map/ppermute | solution.py:26
  285.2 26.6 %collective-permute-start.39 = (bf16[128,512]{1,0:T(8,128)(2,1)S(1)}, bf16[128,512]{1,0:T(8,128)(2,1)S(1)}, u32[]{:S(2)}, u32[]{:S(2)}) collective-permute-start(bf16[128,512]{1,0:T(8,128)(2,1)S(1)} %get-tuple-element.23), channel_id=1, source_target_pairs={{0,1},{1,0},{2,3},{3,2},{4,5},{5,4},{6,7},{7,6},{8,9},{9,8},{10,11... | collective-permute-start | bytes 393224 | tf_op jit(solution)/shard_map/ppermute | solution.py:26
  308.9 20.3 %collective-permute-start.24 = (bf16[256,1024]{1,0:T(8,128)(2,1)S(1)}, bf16[256,1024]{1,0:T(8,128)(2,1)S(1)}, u32[]{:S(2)}, u32[]{:S(2)}) collective-permute-start(bf16[256,1024]{1,0:T(8,128)(2,1)S(1)} %broadcast_select_fusion.10), channel_id=1, source_target_pairs={{0,3},{1,2},{2,1},{3,0},{4,7},{5,6},{6,5},{7,4},{8,11},{9,10},{10,... | collective-permute-start | bytes 1572872 | tf_op jit(solution)/shard_map/ppermute | solution.py:26
  311.9 7.7 %collective-permute-start.42 = (bf16[4,128,512]{2,1,0:T(8,128)(2,1)S(1)}, bf16[4,128,512]{2,1,0:T(8,128)(2,1)S(1)}, u32[]{:S(2)}, u32[]{:S(2)}) collective-permute-start(bf16[4,128,512]{2,1,0:T(8,128)(2,1)S(1)} %pad_maximum_fusion.8), channel_id=1, source_target_pairs={{0,32},{32,0},{64,96},{96,64},{1,33},{33,1},{65,97},{97,65},{2,34}... | collective-permute-start | bytes 1572872 | tf_op jit(solution)/shard_map/ppermute | solution.py:40
  315.8 15.2 %collective-permute-start.23 = (bf16[256,1024]{1,0:T(8,128)(2,1)S(1)}, bf16[256,1024]{1,0:T(8,128)(2,1)S(1)}, u32[]{:S(2)}, u32[]{:S(2)}) collective-permute-start(bf16[256,1024]{1,0:T(8,128)(2,1)S(1)} %broadcast_select_fusion.10), channel_id=1, source_target_pairs={{0,2},{1,3},{2,0},{3,1},{4,6},{5,7},{6,4},{7,5},{8,10},{9,11},{10,... | collective-permute-start | bytes 1572872 | tf_op jit(solution)/shard_map/ppermute | solution.py:26
  315.9 24.4 %collective-permute-start.22 = (bf16[256,1024]{1,0:T(8,128)(2,1)S(1)}, bf16[256,1024]{1,0:T(8,128)(2,1)S(1)}, u32[]{:S(2)}, u32[]{:S(2)}) collective-permute-start(bf16[256,1024]{1,0:T(8,128)(2,1)S(1)} %broadcast_select_fusion.10), channel_id=1, source_target_pairs={{0,1},{1,0},{2,3},{3,2},{4,5},{5,4},{6,7},{7,6},{8,9},{9,8},{10,11... | collective-permute-start | bytes 1572872 | tf_op jit(solution)/shard_map/ppermute | solution.py:26
